TPU v7x, 32 devices: a whole 2x2x4 slice. The times are simulated.
32 devices in a mesh: groups: 2 (over y), tm: 8 (over z, x), chan: 2 (over core).
Axes of the slice: x: 2, y: 2, z: 4, core: 2. Of those that a mesh axis runs over, the one named last changes fastest.
Arguments:
- series: bfloat16 [24576, 512], P(('groups', 'tm'), 'chan'), parts along dimension 0, may hold values from -6 to 6
- cotangent: bfloat16 [24576, 512], P(('groups', 'tm'), 'chan'), parts along dimension 0, may hold values from -3 to 3
- mode_index: int32 [1024], replicated, may hold values from 0 to 6143, as said below
- mix_weight: bfloat16 [2, 1024, 64, 512], P(None, 'tm', None, 'chan'), may hold values from -0.5 to 0.5
Outputs:
- activated: bfloat16 [24576, 512], P(('groups', 'tm'), 'chan'), parts along dimension 0
- series_grad: bfloat16 [24576, 512], P(('groups', 'tm'), 'chan'), parts along dimension 0
- weight_grad: float32 [4, 1024, 64, 512], P('groups', 'tm', None, 'chan'), parts along dimension 0
There are 2 independent parts, one for each index of `groups`. A program takes and returns all parts, laid end to end along the dimension named above; an argument that names none is the same for every part. Nothing has to cross between parts.
Inputs may be any that keep to these rules, and one draw needn't show every extreme that they name: `mode_index`: the 1024 frequencies are distinct; 0 and 6143 are always among them.
All inputs are finite; a program needn't handle non-finite values.
Results may differ from a plain program's by a relative error of at most 0.0074.
Values may be sent and summed in bfloat16 or wider, within the bound.
A program may use at most 192 MiB of HBM per device.

v0:
```python
import math

import jax
import jax.numpy as jnp
from jax import lax
from jax.sharding import PartitionSpec as P


def phase_table(mode_index, first_step, row_count, time_total):
    time_steps = first_step + jnp.arange(row_count, dtype=jnp.int32)
    high_part = (time_steps // 1024)[:, None]
    low_part = (time_steps % 1024)[:, None]
    frequency = mode_index[None, :]
    low_term = frequency * low_part % time_total
    high_term = frequency * high_part % time_total * 1024 % time_total
    residue = (low_term + high_term) % time_total
    phase_angle = residue.astype(jnp.float32) * (2.0 * math.pi / time_total)
    return (jnp.cos(phase_angle).astype(jnp.bfloat16), jnp.sin(phase_angle).astype(jnp.bfloat16))


def transform(signal, cos_table, sin_table, factor):
    dims = (((0,), (0,)), ((), ()))
    real_part = lax.dot_general(cos_table, signal, dims, preferred_element_type=jnp.float32)
    imag_part = lax.dot_general(sin_table, signal, dims, preferred_element_type=jnp.float32)
    return jnp.stack([real_part * factor, -imag_part * factor], axis=1)


def combine(spectrum, cos_table, sin_table, factor):
    first_dot = jnp.dot(cos_table, spectrum[:, 0], preferred_element_type=jnp.float32)
    second_dot = jnp.dot(sin_table, spectrum[:, 1], preferred_element_type=jnp.float32)
    return factor * (first_dot - second_dot)


def activate(pre_act):
    return jax.nn.gelu(pre_act, approximate=True)


def split_parts(spectrum, block_size):
    mode_rows, _, chan_width = spectrum.shape
    block_count = chan_width // block_size
    real_part = spectrum[:, 0].reshape(mode_rows, block_count, block_size)
    imag_part = spectrum[:, 1].reshape(mode_rows, block_count, block_size)
    return (real_part, imag_part)


def split_weight(weight):
    mode_rows, block_size, chan_width = (weight.shape[1], weight.shape[2], weight.shape[3])
    block_count = chan_width // block_size
    weight_real = weight[0].reshape(mode_rows, block_size, block_count, block_size)
    weight_imag = weight[1].reshape(mode_rows, block_size, block_count, block_size)
    return (weight_real, weight_imag)


def product(form, left_side, right_side):
    return jnp.einsum(form, left_side, right_side, preferred_element_type=jnp.float32)


def mix(spectrum, weight):
    mode_rows, _, chan_width = spectrum.shape
    real_part, imag_part = split_parts(spectrum, weight.shape[2])
    weight_real, weight_imag = split_weight(weight)
    out_real = product("mbi,mibj->mbj", real_part, weight_real) - product(
        "mbi,mibj->mbj", imag_part, weight_imag
    )
    out_imag = product("mbi,mibj->mbj", real_part, weight_imag) + product(
        "mbi,mibj->mbj", imag_part, weight_real
    )
    return jnp.stack(
        [out_real.reshape(mode_rows, chan_width), out_imag.reshape(mode_rows, chan_width)], axis=1
    ).astype(jnp.bfloat16)


def mix_grads(spectrum, weight, grad_spec):
    mode_rows, _, chan_width = spectrum.shape
    block_size = weight.shape[2]
    real_part, imag_part = split_parts(spectrum, block_size)
    grad_real, grad_imag = split_parts(grad_spec, block_size)
    weight_real, weight_imag = split_weight(weight)
    dw_real = product("mbi,mbj->mibj", real_part, grad_real) + product(
        "mbi,mbj->mibj", imag_part, grad_imag
    )
    dw_imag = product("mbi,mbj->mibj", real_part, grad_imag) - product(
        "mbi,mbj->mibj", imag_part, grad_real
    )
    weight_grad = jnp.stack(
        [
            dw_real.reshape(mode_rows, block_size, chan_width),
            dw_imag.reshape(mode_rows, block_size, chan_width),
        ],
        axis=0,
    )
    dx_real = product("mibj,mbj->mbi", weight_real, grad_real) + product(
        "mibj,mbj->mbi", weight_imag, grad_imag
    )
    dx_imag = product("mibj,mbj->mbi", weight_real, grad_imag) - product(
        "mibj,mbj->mbi", weight_imag, grad_real
    )
    grad_spectrum = jnp.stack(
        [dx_real.reshape(mode_rows, chan_width), dx_imag.reshape(mode_rows, chan_width)], axis=1
    ).astype(jnp.bfloat16)
    return (weight_grad, grad_spectrum)


def body(series, cotangent, mode_index, mix_weight):
    time_rows = series.shape[0]
    chan_width = series.shape[1]
    time_total = time_rows * lax.axis_size("tm")
    mode_count = mode_index.shape[0]
    owned_modes = mix_weight.shape[1]
    my_rank = lax.axis_index("tm")
    cos_table, sin_table = phase_table(mode_index, my_rank * time_rows, time_rows, time_total)
    scale_in = 1.0 / math.sqrt(time_total)
    scale_out = math.sqrt(2.0 / mode_count)

    def partials(signal, factor):
        return transform(signal, cos_table, sin_table, factor)

    def accumulate(factor, running, piece_modes):
        return running + combine(piece_modes, cos_table, sin_table, factor)

    whole_spectrum = lax.psum(partials(series, scale_in), "tm")
    spectrum = lax.dynamic_slice_in_dim(whole_spectrum, my_rank * owned_modes, owned_modes, 0)
    spectrum_low = spectrum.astype(jnp.bfloat16)
    mixed = mix(spectrum_low, mix_weight)
    empty_field = jnp.zeros((time_rows, chan_width), jnp.float32)
    inverse = accumulate(scale_out, empty_field, lax.all_gather(mixed, "tm", axis=0, tiled=True))
    pre_act = series.astype(jnp.float32) + inverse
    activated, pullback = jax.vjp(activate, pre_act)
    grad_pre = pullback(cotangent.astype(jnp.float32))[0]
    grad_low = grad_pre.astype(jnp.bfloat16)
    whole_grad = lax.psum(partials(grad_low, scale_out), "tm")
    grad_mixed = lax.dynamic_slice_in_dim(whole_grad, my_rank * owned_modes, owned_modes, 0)
    grad_mixed_low = grad_mixed.astype(jnp.bfloat16)
    weight_grad, grad_spectrum = mix_grads(spectrum_low, mix_weight, grad_mixed_low)
    series_grad = accumulate(
        scale_in, grad_pre, lax.all_gather(grad_spectrum, "tm", axis=0, tiled=True)
    )
    return (activated.astype(jnp.bfloat16), series_grad.astype(jnp.bfloat16), weight_grad)


def solution(mesh):
    in_specs = (
        P(("groups", "tm"), "chan"),
        P(("groups", "tm"), "chan"),
        P(),
        P(None, "tm", None, "chan"),
    )
    out_specs = (
        P(("groups", "tm"), "chan"),
        P(("groups", "tm"), "chan"),
        P("groups", "tm", None, "chan"),
    )
    return jax.shard_map(body, mesh=mesh, in_specs=in_specs, out_specs=out_specs, check_vma=False)
```

profile of v0, /device:TPU:0, one launch (start us, length us, event | category | flops | bytes accessed | tf_op | source)
XLA Modules:
  0.0 605.6 jit_solution(9096099381070785772)
XLA Ops:
  7.2 0.0 all-gather.3.cloned.1.call-start
  7.2 0.0 copy-start.4
  7.2 0.0 copy-start.6
  7.3 37.3 %fusion.52 = f32[1024,1,256]{2,0,1:T(8,128)S(1)} fusion(bf16[1536,256]{1,0:T(8,128)(2,1)} %param.4, s32[1536]{0:T(1024)S(1)} %get-tuple-element.32, s32[1536]{0:T(1024)S(1)} %get-tuple-element.33, s32[1024]{0:T(1024)} %param.6), kind=kOutput, calls=%fused_computation.78 | convolution fusion | flops 854589440 | bytes 1851392 | tf_op jit(solution)/shard_map/dot_general | solution.py:24
  44.6 0.0 copy-done.4
  44.6 0.0 copy-done.6
  44.6 0.0 copy-start
  44.6 36.9 %fusion.54 = f32[1024,1,256]{2,0,1:T(8,128)} fusion(bf16[1536,256]{1,0:T(8,128)(2,1)S(1)} %copy-done.4, s32[1536]{0:T(1024)S(1)} %get-tuple-element.32, s32[1536]{0:T(1024)S(1)} %get-tuple-element.33, s32[1024]{0:T(1024)S(1)} %copy-done.6), kind=kOutput, calls=%fused_computation.80 | convolution fusion | flops 854327296 | bytes 1851392 | tf_op jit(solution)/shard_map/dot_general | solution.py:23
  81.5 0.0 copy-done
  81.5 3.9 fusion.98
  85.4 6.9 %copy.70 = bf16[1,128,64,256]{1,3,2,0:T(8,128)(2,1)} copy(bf16[1,128,64,256]{3,2,1,0:T(8,128)(2,1)} %get-tuple-element.19) | data formatting | bytes 8388608
  92.3 1.4 pad_maximum_fusion.1
  93.7 95.5 %all-reduce.2 = bf16[1024,2,256]{2,0,1:T(8,128)(2,1)S(1)} all-reduce(f32[1024,2,256]{2,0,1:T(8,128)S(1)} %pad_maximum_fusion.1), channel_id=1, replica_groups=mesh['groups'=2,'tm'=8,'chan'=2] {'tm'}, use_global_device_ids=true, to_apply=%region_0.1 | all-reduce | flops 524288 | bytes 3145728 | tf_op jit(solution)/shard_map/psum | solution.py:121
  189.2 0.1 copy.9
  189.4 0.1 copy.72
  189.4 0.1 copy.11
  189.5 0.1 copy.73
  189.6 6.9 %copy.71 = bf16[1,128,64,256]{1,3,2,0:T(8,128)(2,1)} copy(bf16[1,128,64,256]{3,2,1,0:T(8,128)(2,1)} %get-tuple-element.18) | data formatting | bytes 8388608
  196.5 5.0 fusion
  201.6 0.7 pad_maximum_fusion.3
  202.3 0.0 all-gather.3.cloned.1.call-update
  202.3 0.0 copy-start.3
  202.4 0.0 copy-start.5
  202.4 0.0 all-gather.5.cloned.1.call-start
  202.4 37.0 %all-gather.3.cloned.1.call-done = bf16[1024,2,256]{0,2,1:T(8,128)(2,1)} async-done(((bf16[128,2,256]{0,2,1:T(8,128)(2,1)}), bf16[1024,2,256]{0,2,1:T(8,128)(2,1)}) %all-gather.3.cloned.1.call-update) | async-done | bytes 1048592 | tf_op jit(solution)/shard_map/all_gather | solution.py:126
  239.5 35.9 %fusion.25 = f32[1536,256]{1,0:T(8,128)S(1)} fusion(s32[1536]{0:T(1024)S(1)} %get-tuple-element.32, s32[1536]{0:T(1024)S(1)} %get-tuple-element.33, s32[1024]{0:T(1024)S(1)} %copy-done.6, bf16[1024,2,256]{0,2,1:T(8,128)(2,1)} %all-gather.3.cloned.1.call-done), kind=kOutput, calls=%fused_computation.44 | convolution fusion | flops 854065152 | bytes 2113536 | tf_op jit(solution)/shard_map/dot_general | solution.py:29
  275.3 0.0 copy-done.3
  275.3 0.0 copy-done.5
  275.3 0.0 copy-done.2
  275.4 37.3 %fusion.39 = (f32[1536,256]{1,0:T(8,128)S(1)}, bf16[1536,256]{1,0:T(8,128)(2,1)}) fusion(bf16[1536,256]{1,0:T(8,128)(2,1)S(1)} %copy-done.3, f32[1536,256]{1,0:T(8,128)S(1)} %fusion.25, bf16[1024,2,256]{0,2,1:T(8,128)(2,1)S(1)} %copy-done.2, s32[1536]{0:T(1024)S(1)} %get-tuple-element.32, s32[1536]{0:T(1024)S(1)} %get-tuple-element.33, ...), kind=kOutput, calls=%fused_computation.64 | convolution fusion | flops 864288768 | bytes 6049792 | tf_op jit(solution)/shard_map/dot_general | solution.py:30
  312.7 0.0 copy-start.7
  312.7 35.7 %fusion.50 = f32[1024,1,256]{2,0,1:T(8,128)S(1)} fusion(s32[1536]{0:T(1024)S(1)} %get-tuple-element.32, s32[1536]{0:T(1024)S(1)} %get-tuple-element.33, s32[1024]{0:T(1024)S(1)} %copy-done.6, f32[1536,256]{1,0:T(8,128)S(1)} %get-tuple-element.20), kind=kOutput, calls=%fused_computation.76 | convolution fusion | flops 854982656 | bytes 2637824 | tf_op jit(solution)/shard_map/dot_general | solution.py:24
  348.4 0.0 copy-done.7
  348.4 35.7 %fusion.56 = f32[1024,1,256]{2,0,1:T(8,128)S(1)} fusion(s32[1536]{0:T(1024)S(1)} %get-tuple-element.32, s32[1536]{0:T(1024)S(1)} %get-tuple-element.33, s32[1024]{0:T(1024)S(1)} %copy-done.6, f32[1536,256]{1,0:T(8,128)S(1)} %get-tuple-element.20), kind=kOutput, calls=%fused_computation.82 | convolution fusion | flops 854720512 | bytes 2637824 | tf_op jit(solution)/shard_map/dot_general | solution.py:23
  384.1 0.1 pad_maximum_fusion.2
  384.3 91.9 %all-reduce.3 = bf16[1024,2,256]{2,0,1:T(8,128)(2,1)S(1)} all-reduce(f32[1024,2,256]{2,0,1:T(8,128)S(1)} %pad_maximum_fusion.2), channel_id=1, replica_groups=mesh['groups'=2,'tm'=8,'chan'=2] {'tm'}, use_global_device_ids=true, to_apply=%region_1.2 | all-reduce | flops 524288 | bytes 3145728 | tf_op jit(solution)/shard_map/psum | solution.py:131
  476.3 0.1 copy.14
  476.4 0.1 copy.13
  476.5 12.8 %multiply_add_fusion = (f32[128,4,64,64]{0,2,1,3:T(8,128)}, f32[128,4,64,64]{0,2,1,3:T(8,128)}, f32[128,4,64]{0,1,2:T(4,128)S(1)}, f32[128,4,64]{0,1,2:T(4,128)S...) fusion(f32[128,4,64]{0,2,1:T(8,128)S(1)} %convert.50, f32[128,4,64]{0,2,1:T(8,128)S(1)} %convert.48, ...), kind=kLoop, calls=%fused_computation.22 | loop fusion | flops 33423360 | bytes 26214400 | tf_op jit(solution)/shard_map/add | solution.py:79
  489.4 0.7 pad_maximum_fusion.4
  490.0 0.0 all-gather.5.cloned.1.call-update
  490.1 11.7 %pad_maximum_fusion = f32[2,128,64,256]{1,3,2,0:T(8,128)} fusion(f32[1,128,64,256]{1,3,2,0:T(8,128)} %bitcast.78, f32[1,128,64,256]{1,3,2,0:T(8,128)} %bitcast.77), kind=kLoop, calls=%fused_computation | loop fusion | flops 4194304 | bytes 33554432 | tf_op jit(solution)/shard_map/stack | solution.py:85
  501.7 17.4 %copy.17 = f32[2,128,64,256]{3,2,1,0:T(8,128)} copy(f32[2,128,64,256]{1,3,2,0:T(8,128)} %pad_maximum_fusion) | data formatting | bytes 33554432
  519.1 8.0 %all-gather.5.cloned.1.call-done = bf16[1024,2,256]{0,2,1:T(8,128)(2,1)} async-done(((bf16[128,2,256]{0,2,1:T(8,128)(2,1)}), bf16[1024,2,256]{0,2,1:T(8,128)(2,1)}) %all-gather.5.cloned.1.call-update) | async-done | bytes 1048592 | tf_op jit(solution)/shard_map/all_gather | solution.py:136
  527.1 35.9 %fusion.23 = f32[1536,256]{1,0:T(8,128)S(1)} fusion(s32[1536]{0:T(1024)S(1)} %get-tuple-element.32, s32[1536]{0:T(1024)S(1)} %get-tuple-element.33, s32[1024]{0:T(1024)S(1)} %copy-done.6, bf16[1024,2,256]{0,2,1:T(8,128)(2,1)} %all-gather.5.cloned.1.call-done), kind=kOutput, calls=%fused_computation.42 | convolution fusion | flops 854065152 | bytes 2113536 | tf_op jit(solution)/shard_map/dot_general | solution.py:29
  563.0 0.0 copy-done.8
  563.0 0.0 copy-done.1
  563.0 35.6 %fusion.37 = bf16[1536,256]{1,0:T(8,128)(2,1)} fusion(f32[1536,256]{1,0:T(8,128)S(1)} %copy-done.8, f32[1536,256]{1,0:T(8,128)S(1)} %fusion.23, s32[1536]{0:T(1024)S(1)} %get-tuple-element.32, s32[1536]{0:T(1024)S(1)} %get-tuple-element.33, s32[1024]{0:T(1024)S(1)} %copy-done.6, bf16[1024,2,256]{0,2,1:T(8,128)(2,1)S(1)} %copy-done.1), kind=kOutput, calls=%fused_computation.56 | convolution fusion | flops 855638016 | bytes 4476928 | tf_op jit(solution)/shard_map/dot_general | solution.py:30
  (14 shorter events, 0.2 us)
Async XLA Ops:
  7.2 232.3 %all-gather.3.cloned.1.call-start = ((), (), s32[]{:S(2)}) async-start(), calls=%async_computation | async-start | bytes 1179648 | tf_op jit(solution)/shard_map/all_gather | solution.py:126
  7.2 37.3 %copy-start.4 = (bf16[1536,256]{1,0:T(8,128)(2,1)S(1)}, bf16[1536,256]{1,0:T(8,128)(2,1)}, u32[]{:S(2)}) copy-start(bf16[1536,256]{1,0:T(8,128)(2,1)} %param.4) | copy-start | bytes 2359300
  7.2 37.3 %copy-start.6 = (s32[1024]{0:T(1024)S(1)}, s32[1024]{0:T(1024)}, u32[]{:S(2)}) copy-start(s32[1024]{0:T(1024)} %param.6) | copy-start | bytes 12292
  44.6 36.9 %copy-start = (bf16[2,128,64,256]{3,2,1,0:T(8,128)(2,1)S(1)}, bf16[2,128,64,256]{3,2,1,0:T(8,128)(2,1)}, u32[]{:S(2)}) copy-start(bf16[2,128,64,256]{3,2,1,0:T(8,128)(2,1)} %param.7) | copy-start | bytes 25165828
  202.3 73.0 %copy-start.3 = (bf16[1536,256]{1,0:T(8,128)(2,1)S(1)}, bf16[1536,256]{1,0:T(8,128)(2,1)}, u32[]{:S(2)}) copy-start(bf16[1536,256]{1,0:T(8,128)(2,1)} %param.5) | copy-start | bytes 2359300
  202.4 73.0 %copy-start.5 = (bf16[1536,256]{1,0:T(8,128)(2,1)S(1)}, bf16[1536,256]{1,0:T(8,128)(2,1)}, u32[]{:S(2)}) copy-start(bf16[1536,256]{1,0:T(8,128)(2,1)} %param.4) | copy-start | bytes 2359300
  202.4 324.7 %all-gather.5.cloned.1.call-start = ((), (), s32[]{:S(2)}) async-start(), calls=%async_computation.1 | async-start | bytes 1179648 | tf_op jit(solution)/shard_map/all_gather | solution.py:136
  239.5 35.9 %copy-start.2 = (bf16[1024,2,256]{0,2,1:T(8,128)(2,1)S(1)}, bf16[1024,2,256]{0,2,1:T(8,128)(2,1)}, u32[]{:S(2)}) copy-start(bf16[1024,2,256]{0,2,1:T(8,128)(2,1)} %all-gather.3.cloned.1.call-done) | copy-start | bytes 3145732
  312.7 35.7 %copy-start.7 = (f32[1536,256]{1,0:T(8,128)}, f32[1536,256]{1,0:T(8,128)S(1)}, u32[]{:S(2)}) copy-start(f32[1536,256]{1,0:T(8,128)S(1)} %get-tuple-element.20) | copy-start | bytes 4718596
  519.1 43.9 %copy-start.8 = (f32[1536,256]{1,0:T(8,128)S(1)}, f32[1536,256]{1,0:T(8,128)}, u32[]{:S(2)}) copy-start(f32[1536,256]{1,0:T(8,128)} %copy-done.7) | copy-start | bytes 4718596
  527.1 35.9 %copy-start.1 = (bf16[1024,2,256]{0,2,1:T(8,128)(2,1)S(1)}, bf16[1024,2,256]{0,2,1:T(8,128)(2,1)}, u32[]{:S(2)}) copy-start(bf16[1024,2,256]{0,2,1:T(8,128)(2,1)} %all-gather.5.cloned.1.call-done) | copy-start | bytes 3145732
Sparse Core Ops, SparseCore 0:
  202.5 36.9 all-gather.2
  490.2 36.8 all-gather.4
where the time goes:
time: 611 us; the launch traced here: 606 us
  matrix products  290 us (47%)
  blocking collectives  187 us (31%)
  waiting for transfers between devices  45.1 us (7%)
  local copies, waits for them, and re-layouts  35.8 us (6%)
  other arithmetic  32.4 us (5%)
  between operations  14.6 us (2%)
    psum x1, blocking collectives, body(): whole_spectrum = lax.psum(partials(series, scale_in), 'tm')  95.5 us
    psum x1, blocking collectives, body(): whole_grad = lax.psum(partials(grad_low, scale_out), 'tm')  91.9 us
    dot_general x2, matrix products, transform(): lax.dot_general(sin_table, signal, dims, preferred_element_type=jnp.float32)  73 us
    dot_general x2, matrix products, combine(): jnp.dot(sin_table, spectrum[:, 1], preferred_element_type=jnp.float32)  73 us
    dot_general x2, matrix products, transform(): lax.dot_general(cos_table, signal, dims, preferred_element_type=jnp.float32)  72.6 us
    dot_general x2, matrix products, combine(): jnp.dot(cos_table, spectrum[:, 0], preferred_element_type=jnp.float32)  71.7 us
    all_gather x1, waiting for transfers between devices, body(): lax.all_gather(mixed, 'tm', axis=0, tiled=True)  37 us
    unnamed x23, local copies, waits for them, and re-layouts  31.4 us
  transfers between devices with their start and end apart: 2, of which 2 were waited for; matrix products, arithmetic and copies ran while one was open for 5% of the time, Pallas kernels for 0%

commit v1 on v0

v1 whole, which is shorter than its diff:
```python
import functools
import math

import jax
import jax.numpy as jnp
from jax import lax
from jax.experimental import pallas as pl
from jax.experimental.pallas import tpu as pltpu
from jax.sharding import PartitionSpec as P

LANES = 128
FINE = 16
MODES_PER_STEP = 8
VMEM_BYTES = 56 * 1024 * 1024
F32 = jnp.float32
BF16 = jnp.bfloat16


def base_tables(mode_index, first_step, device_count, time_total):
    owned = mode_index.shape[0] // device_count
    frequency = mode_index.reshape(device_count, 1, owned)
    frequency = jnp.broadcast_to(frequency, (device_count, 2, owned)).reshape(1, -1)
    quarter = jnp.arange(2, dtype=jnp.int32).reshape(1, 2, 1) * (time_total // 4)
    quarter = jnp.broadcast_to(quarter, (device_count, 2, owned)).reshape(1, -1)
    row = jnp.arange(32, dtype=jnp.int32)
    steps = jnp.where(row < FINE, row, (row - FINE) * FINE)
    steps = jnp.where(row == 24, first_step, steps)
    steps = jnp.where(row == 25, first_step + LANES, steps)
    steps = jnp.where(row == 26, LANES, steps)
    steps = jnp.where(row > 26, 0, steps)[:, None]
    low_term = frequency * (steps % 1024) % time_total
    high_term = frequency * (steps // 1024) % time_total * 1024 % time_total
    shift = jnp.where((row[:, None] == 24) | (row[:, None] == 25), quarter, 0)
    residue = (low_term + high_term + shift) % time_total
    angle = residue.astype(F32) * (2.0 * math.pi / time_total)
    return jnp.cos(angle), jnp.sin(angle)


def start_blocks(cos_ref, sin_ref, lanes):
    fine_cos, fine_sin = cos_ref[0:FINE, lanes], sin_ref[0:FINE, lanes]
    first, second = [], []
    for coarse in range(FINE, FINE + LANES // FINE):
        coarse_cos, coarse_sin = cos_ref[coarse : coarse + 1, lanes], sin_ref[coarse : coarse + 1, lanes]
        step_cos = coarse_cos * fine_cos - coarse_sin * fine_sin
        step_sin = coarse_sin * fine_cos + coarse_cos * fine_sin
        first.append(cos_ref[24:25, lanes] * step_cos - sin_ref[24:25, lanes] * step_sin)
        second.append(cos_ref[25:26, lanes] * step_cos - sin_ref[25:26, lanes] * step_sin)
    turn = 2.0 * cos_ref[26:27, lanes]
    turn = jnp.broadcast_to(turn, (LANES, LANES))
    return jnp.concatenate(first, axis=0), jnp.concatenate(second, axis=0), turn


def lane_block(index):
    return pl.ds(pl.multiple_of(index * LANES, LANES), LANES)


def fill_tables(cos_ref, sin_ref, table, table_t):
    step_blocks = (table if table is not None else table_t).shape[0 if table is not None else 1] // LANES

    def chunk(index, carry):
        lanes = lane_block(index)
        before, now, turn = start_blocks(cos_ref, sin_ref, lanes)
        if table is None:
            before, now, turn = before.T, now.T, turn.T
        for block in range(step_blocks):
            place = slice(block * LANES, (block + 1) * LANES)
            if table is None:
                table_t[lanes, place] = before.astype(BF16)
            else:
                table[place, lanes] = before.astype(BF16)
            before, now = now, turn * now - before
        return carry

    lax.fori_loop(0, cos_ref.shape[1] // LANES, chunk, 0)


def block_masks(block_size, width):
    row = lax.broadcasted_iota(jnp.int32, (block_size, width), 0)
    column = lax.broadcasted_iota(jnp.int32, (block_size, width), 1)
    pick = column % block_size == row
    left = lax.broadcasted_iota(jnp.int32, (width, width), 0) // block_size
    right = lax.broadcasted_iota(jnp.int32, (width, width), 1) // block_size
    return pick, (left == right).astype(F32).astype(BF16)


def spread_rows(ref, first_row, block_size):
    rows = [
        jnp.broadcast_to(ref[pl.ds(first_row + k, 1), :], (block_size, ref.shape[1]))
        for k in range(MODES_PER_STEP)
    ]
    return jnp.concatenate(rows, axis=0)


def expand(ref, first_row, pick, same_block):
    rows = spread_rows(ref, first_row, pick.shape[0])
    rows = jnp.where(jnp.concatenate([pick] * MODES_PER_STEP, axis=0), rows, 0.0).astype(BF16)
    return jnp.dot(rows, same_block, preferred_element_type=F32)


def fold(values, block_size):
    return values.reshape(MODES_PER_STEP, block_size, values.shape[1]).sum(axis=1)


def mode_weights(weight, part, first_row):
    rows = weight[part, pl.ds(first_row, MODES_PER_STEP)]
    return rows.reshape(rows.shape[0] * rows.shape[1], rows.shape[2]).astype(F32)


def spectral_kernel(
    scale_in,
    scale_out,
    count,
    cos_ref,
    sin_ref,
    series,
    cotangent,
    weight_hbm,
    activated,
    series_grad,
    spectrum_out,
    grad_out,
    weight,
    table,
    table_t,
    field,
    grad_pre,
    grad_low,
    partial,
    pair_in,
    pair_sum,
    line_in,
    gathered,
    spectrum,
    rows_out,
    weight_sem,
    pair_send,
    pair_recv,
    line_send,
    line_recv,
    share_send,
    share_recv,
    cross_send,
    cross_recv,
):
    half = count // 2
    owned = weight.shape[1]
    block_size = weight.shape[2]
    rows = 2 * owned
    time_rows, width = series.shape
    me = lax.axis_index("tm")
    high, low = me // 2, me % 2
    partner = high * 2 + 1 - low

    def peer(offset):
        return lax.rem(high + offset, half) * 2 + low

    def block(device):
        return pl.ds(pl.multiple_of(device * rows, rows), rows)

    def copy(source, target, send_sem, recv_sem, device):
        return pltpu.make_async_remote_copy(
            src_ref=source,
            dst_ref=target,
            send_sem=send_sem,
            recv_sem=recv_sem,
            device_id={"tm": device},
            device_id_type=pl.DeviceIdType.MESH,
        )

    load = pltpu.make_async_copy(weight_hbm, weight, weight_sem)
    load.start()
    barrier = pltpu.get_barrier_semaphore()
    pl.semaphore_signal(barrier, inc=1, device_id={"tm": partner}, device_id_type=pl.DeviceIdType.MESH)

    def greet(offset, carry):
        pl.semaphore_signal(barrier, inc=1, device_id={"tm": peer(offset)}, device_id_type=pl.DeviceIdType.MESH)
        return carry

    lax.fori_loop(1, half, greet, 0)

    def reduce_scatter(phase, signal, factor, meanwhile):
        def pair_copy(k):
            target = lax.rem(high + 1 + k, half) * 2 + 1 - low
            return copy(
                partial.at[phase, block(target)],
                pair_in.at[phase, k],
                pair_send.at[phase, k],
                pair_recv.at[phase, k],
                partner,
            )

        def line_copy(k):
            return copy(
                pair_sum.at[phase, k],
                line_in.at[phase, k],
                line_send.at[phase, k],
                line_recv.at[phase, k],
                peer(k + 1),
            )

        def project(device):
            product = jnp.dot(table_t[block(device), :], signal[...], preferred_element_type=F32)
            partial[phase, block(device), :] = (product * factor).astype(BF16)

        def send_pair(k, carry):
            project(lax.rem(high + 1 + k, half) * 2 + 1 - low)
            pair_copy(k).start()
            return carry

        lax.fori_loop(0, half, send_pair, 0)

        def own_part(k, carry):
            project(peer(k + 1))
            return carry

        lax.fori_loop(0, half, own_part, 0)

        def send_line(k, carry):
            pair_copy(k).wait_recv()
            own = partial[phase, block(peer(k + 1)), :].astype(F32)
            pair_sum[phase, k] = (own + pair_in[phase, k].astype(F32)).astype(BF16)
            line_copy(k).start()
            return carry

        lax.fori_loop(0, half - 1, send_line, 0)
        meanwhile()
        pair_copy(half - 1).wait_recv()
        total = partial[phase, block(me), :].astype(F32) + pair_in[phase, half - 1].astype(F32)

        def add(k, total):
            line_copy(k).wait_recv()
            return total + line_in[phase, k].astype(F32)

        for k in range(half - 1) if half <= 8 else ():
            total = add(k, total)
        if half > 8:
            total = lax.fori_loop(0, half - 1, add, total)
        spectrum[phase] = total.astype(BF16).astype(F32)

        def done(k, carry):
            pair_copy(k).wait_send()
            return carry

        lax.fori_loop(0, half, done, 0)

        def done_line(k, carry):
            line_copy(k).wait_send()
            return carry

        lax.fori_loop(0, half - 1, done_line, 0)

    def add_block(phase, first_row, depth, begin):
        place = pl.ds(pl.multiple_of(first_row, depth), depth)
        right = gathered[phase, place, :]

        def tile(t, carry):
            steps = pl.ds(pl.multiple_of(t * 2 * LANES, 2 * LANES), 2 * LANES)
            product = jnp.dot(table[steps, place], right, preferred_element_type=F32)
            if begin:
                field[steps, :] = product
            else:
                field[steps, :] += product
            return carry

        lax.fori_loop(0, time_rows // (2 * LANES), tile, 0)

    def gather(phase):
        early = rows % LANES == 0

        def share_copy(k):
            return copy(
                gathered.at[phase, block(me)],
                gathered.at[phase, block(me)],
                share_send.at[phase, k],
                share_recv.at[phase, k],
                peer(k),
            )

        def cross_copy(k):
            held = block(lax.rem(high - k + half, half) * 2 + low)
            return copy(
                gathered.at[phase, held],
                gathered.at[phase, held],
                cross_send.at[phase, k],
                cross_recv.at[phase, k],
                partner,
            )

        def arrival(device, recv_sem):
            place = gathered.at[phase, block(device)]
            return copy(place, place, recv_sem, recv_sem, partner)

        gathered[phase, block(me), :] = rows_out[...].astype(BF16)
        cross_copy(0).start()

        def share(k, carry):
            share_copy(k).start()
            return carry

        lax.fori_loop(1, half, share, 0)
        if early:
            add_block(phase, me * rows, rows, True)

        def forward(k, carry):
            device = lax.rem(high - k + half, half) * 2 + low
            arrival(device, share_recv.at[phase, k]).wait_recv()
            cross_copy(k).start()
            if early:
                add_block(phase, device * rows, rows, False)
            return carry

        lax.fori_loop(1, half, forward, 0)

        def receive(k, carry):
            device = lax.rem(high - k + half, half) * 2 + 1 - low
            arrival(device, cross_recv.at[phase, k]).wait_recv()
            if early:
                add_block(phase, device * rows, rows, False)
            return carry

        lax.fori_loop(0, half, receive, 0)
        if not early:
            depth = 2 * LANES
            add_block(phase, 0, depth, True)

            def rest(unit, carry):
                add_block(phase, unit * depth, depth, False)
                return carry

            lax.fori_loop(1, count * rows // depth, rest, 0)

        def done(k, carry):
            share_copy(k).wait_send()
            cross_copy(k).wait_send()
            return carry

        lax.fori_loop(1, half, done, 0)
        cross_copy(0).wait_send()

    pick, same_block = block_masks(block_size, width)

    def mix(step, carry):
        first = pl.multiple_of(step * MODES_PER_STEP, MODES_PER_STEP)
        second = pl.multiple_of(owned + step * MODES_PER_STEP, MODES_PER_STEP)
        x_real = expand(spectrum.at[0], first, pick, same_block)
        x_imag = expand(spectrum.at[0], second, pick, same_block)
        w_real, w_imag = mode_weights(weight, 0, first), mode_weights(weight, 1, first)
        rows_out[pl.ds(first, MODES_PER_STEP), :] = fold(x_real * w_real - x_imag * w_imag, block_size)
        rows_out[pl.ds(second, MODES_PER_STEP), :] = fold(x_real * w_imag + x_imag * w_real, block_size)
        return carry

    def mix_back(step, carry):
        first = pl.multiple_of(step * MODES_PER_STEP, MODES_PER_STEP)
        second = pl.multiple_of(owned + step * MODES_PER_STEP, MODES_PER_STEP)
        g_real = spread_rows(spectrum.at[1], first, block_size)
        g_imag = spread_rows(spectrum.at[1], second, block_size)
        w_real, w_imag = mode_weights(weight, 0, first), mode_weights(weight, 1, first)
        chosen = jnp.concatenate([pick] * MODES_PER_STEP, axis=0)

        def gathered_rows(values):
            sums = jnp.dot(values.astype(BF16), same_block, preferred_element_type=F32)
            return fold(jnp.where(chosen, sums, 0.0), block_size)

        rows_out[pl.ds(first, MODES_PER_STEP), :] = gathered_rows(w_real * g_real + w_imag * g_imag)
        rows_out[pl.ds(second, MODES_PER_STEP), :] = gathered_rows(w_real * g_imag - w_imag * g_real)
        return carry

    fill_tables(cos_ref, sin_ref, None, table_t)
    pl.semaphore_wait(barrier, half)
    reduce_scatter(0, series, scale_in, lambda: fill_tables(cos_ref, sin_ref, table, None))
    load.wait()
    lax.fori_loop(0, owned // MODES_PER_STEP, mix, 0)
    gather(0)

    slope = math.sqrt(2.0 / math.pi)

    def activate(t, carry):
        steps = pl.ds(pl.multiple_of(t * LANES, LANES), LANES)
        value = series[steps, :].astype(F32) + scale_out * field[steps, :]
        square = value * value
        tanh = jnp.tanh(slope * (value + 0.044715 * (square * value)))
        gate = 0.5 * (1.0 + tanh)
        activated[steps, :] = (value * gate).astype(BF16)
        inner = slope * (1.0 + 3.0 * 0.044715 * square)
        derivative = gate + 0.5 * value * (1.0 - tanh * tanh) * inner
        grad = cotangent[steps, :].astype(F32) * derivative
        grad_pre[steps, :] = grad
        grad_low[steps, :] = grad.astype(BF16)
        return carry

    lax.fori_loop(0, time_rows // LANES, activate, 0)
    reduce_scatter(1, grad_low, scale_out, lambda: None)
    lax.fori_loop(0, owned // MODES_PER_STEP, mix_back, 0)
    spectrum_out[...] = spectrum[0]
    grad_out[...] = spectrum[1]
    gather(1)

    def finish(t, carry):
        steps = pl.ds(pl.multiple_of(t * LANES, LANES), LANES)
        series_grad[steps, :] = (grad_pre[steps, :] + scale_in * field[steps, :]).astype(BF16)
        return carry

    lax.fori_loop(0, time_rows // LANES, finish, 0)


def weight_grad_kernel(x_real, x_imag, g_real, g_imag, out):
    block_size, width = out.shape[2], out.shape[3]
    pick, same_block = block_masks(block_size, width)
    shape = (MODES_PER_STEP, block_size, width)
    xr, xi = expand(x_real, 0, pick, same_block), expand(x_imag, 0, pick, same_block)
    gr, gi = spread_rows(g_real, 0, block_size), spread_rows(g_imag, 0, block_size)
    out[0] = (xr * gr + xi * gi).reshape(shape)
    out[1] = (xr * gi - xi * gr).reshape(shape)


def weight_gradient(spectrum, grad, block_size):
    owned, width = spectrum.shape[0] // 2, spectrum.shape[1]
    steps = owned // MODES_PER_STEP
    real = pl.BlockSpec((MODES_PER_STEP, width), lambda g: (g, 0))
    imag = pl.BlockSpec((MODES_PER_STEP, width), lambda g: (g + steps, 0))
    return pl.pallas_call(
        weight_grad_kernel,
        grid=(steps,),
        in_specs=[real, imag, real, imag],
        out_specs=pl.BlockSpec((2, MODES_PER_STEP, block_size, width), lambda g: (0, g, 0, 0)),
        out_shape=jax.ShapeDtypeStruct((2, owned, block_size, width), F32),
        compiler_params=pltpu.CompilerParams(vmem_limit_bytes=VMEM_BYTES),
    )(spectrum, spectrum, grad, grad)


def body(series, cotangent, mode_index, mix_weight):
    time_rows, width = series.shape
    count = lax.axis_size("tm")
    modes = mode_index.shape[0]
    owned = mix_weight.shape[1]
    rows = 2 * owned
    half = count // 2
    time_total = time_rows * count
    cos_base, sin_base = base_tables(mode_index, lax.axis_index("tm") * time_rows, count, time_total)
    kernel = functools.partial(
        spectral_kernel, 1.0 / math.sqrt(time_total), math.sqrt(2.0 / modes), count
    )
    vmem = pl.BlockSpec(memory_space=pltpu.VMEM)
    sems = pltpu.SemaphoreType.DMA((2, half))
    activated, series_grad, spectrum, grad = pl.pallas_call(
        kernel,
        in_specs=[vmem] * 4 + [pl.BlockSpec(memory_space=pl.ANY)],
        out_specs=[vmem] * 4,
        out_shape=[
            jax.ShapeDtypeStruct((time_rows, width), BF16),
            jax.ShapeDtypeStruct((time_rows, width), BF16),
            jax.ShapeDtypeStruct((rows, width), F32),
            jax.ShapeDtypeStruct((rows, width), F32),
        ],
        scratch_shapes=[
            pltpu.VMEM(mix_weight.shape, BF16),
            pltpu.VMEM((time_rows, 2 * modes), BF16),
            pltpu.VMEM((2 * modes, time_rows), BF16),
            pltpu.VMEM((time_rows, width), F32),
            pltpu.VMEM((time_rows, width), F32),
            pltpu.VMEM((time_rows, width), BF16),
            pltpu.VMEM((2, 2 * modes, width), BF16),
            pltpu.VMEM((2, half, rows, width), BF16),
            pltpu.VMEM((2, half, rows, width), BF16),
            pltpu.VMEM((2, half, rows, width), BF16),
            pltpu.VMEM((2, 2 * modes, width), BF16),
            pltpu.VMEM((2, rows, width), F32),
            pltpu.VMEM((rows, width), F32),
            pltpu.SemaphoreType.DMA,
        ]
        + [sems] * 8,
        compiler_params=pltpu.CompilerParams(
            collective_id=0, has_side_effects=True, vmem_limit_bytes=VMEM_BYTES
        ),
    )(cos_base, sin_base, series, cotangent, mix_weight)
    return activated, series_grad, weight_gradient(spectrum, grad, mix_weight.shape[2])


def solution(mesh):
    in_specs = (
        P(("groups", "tm"), "chan"),
        P(("groups", "tm"), "chan"),
        P(),
        P(None, "tm", None, "chan"),
    )
    out_specs = (
        P(("groups", "tm"), "chan"),
        P(("groups", "tm"), "chan"),
        P("groups", "tm", None, "chan"),
    )
    return jax.shard_map(body, mesh=mesh, in_specs=in_specs, out_specs=out_specs, check_vma=False)
```

time: 611 us -> 111 us (0.18)
  matrix products: 290 us -> 0 us
  blocking collectives: 187 us -> 0 us
  Pallas kernels: 0 us -> 104 us
  waiting for transfers between devices: 45.1 us -> 0 us
  local copies, waits for them, and re-layouts: 35.8 us -> 2.53 us
  other arithmetic: 32.4 us -> 2.4 us
  between operations: 14.6 us -> 0.68 us
    dot_general x8 -> x0, matrix products: 290 us -> none  [the longest x2 73 us: transform(): lax.dot_general(sin_table, signal, dims, preferred_element_type=jnp.float32)]
    psum x2 -> x0, blocking collectives: 187 us -> none  [the longest x1 95.5 us: body(): whole_spectrum = lax.psum(partials(series, scale_in), 'tm')]
    pallas_call x0 -> x2, Pallas kernels: none -> 104 us  [the longest x1 91.6 us: body(): pl.pallas_call(kernel, in_specs=[vmem] * 4 + [pl.BlockSpec(memory_space=p...]
    all_gather x2 -> x0, waiting for transfers between devices: 45 us -> none  [the longest x1 37 us: body(): lax.all_gather(mixed, 'tm', axis=0, tiled=True)]
    unnamed x23 -> x6, local copies, waits for them, and re-layouts: 31.4 us -> 1.77 us
    another operation x9 -> x0, other arithmetic: 14.6 us -> none  [the longest x1 11.7 us: mix_grads(): jnp.stack([dw_real.reshape(mode_rows, block_size, chan_width), dw_imag.re...]
    add x1 -> x0, other arithmetic: 12.8 us -> none  [mix_grads(): product('mbi,mbj->mibj', real_part, grad_real)]
  transfers between devices with their start and end apart: 2 -> 0, of which waited for: 2 -> 0; matrix products, arithmetic and copies ran while one was open for 5% -> 0% of each run, Pallas kernels for 0% -> 0%
where the time goes in v1:
time: 111 us; the launch traced here: 110 us
  Pallas kernels  104 us (94%)
  local copies, waits for them, and re-layouts  2.53 us (2%)
  other arithmetic  2.4 us (2%)
    pallas_call x1, Pallas kernels, body(): pl.pallas_call(kernel, in_specs=[vmem] * 4 + [pl.BlockSpec(memory_space=p...  91.6 us
    pallas_call x1, Pallas kernels, weight_gradient(): pl.pallas_call(weight_grad_kernel, grid=(steps,), in_specs=[real, imag, r...  12.4 us
    sin x1, other arithmetic, base_tables(): return (jnp.cos(angle), jnp.sin(angle))  2.37 us

profile of v1, /device:TPU:0, one launch (start us, length us, event | category | flops | bytes accessed | tf_op | source)
XLA Modules:
  0.0 109.7 jit_solution(2429192777981596025)
XLA Ops:
  0.7 0.1 broadcast_in_dim.56
  0.8 0.7 broadcast_in_dim.50
  1.4 2.4 %fusion.16 = (f32[32,2048]{1,0:T(8,128)}, f32[32,2048]{1,0:T(8,128)}) fusion(s32[2048]{0:T(1024)S(1)} %bitcast.3, pred[32]{0:T(512)(128)(4,1)S(1)} %compare_or_fusion, s32[32]{0:T(128)S(1)} %get-tuple-element.13, s32[32]{0:T(128)S(1)} %get-tuple-element.14, s32[2048]{0:T(1024)S(1)} %bitcast.4), kind=kLoop, calls=%fused_computation.22 | loop fusion | flops 2097152 | bytes 540960 | tf_op jit(solution)/shard_map/sin | solution.py:36
  3.8 91.6 %shard_map.67 = (bf16[1536,256]{1,0:T(8,128)(2,1)}, bf16[1536,256]{1,0:T(8,128)(2,1)}, f32[256,256]{1,0:T(8,128)}, f32[256,256]{1,0:T(8,128)}) custom-call(f32[32,2048]{1,0:T(8,128)} %get-tuple-element.12.cos_ref, f32[32,2048]{1,0:T(8,128)} %get-tuple-element.11.sin_ref, bf16[1536,256]{1,0:T(8,128)(2,1)} %series.1, bf16[1536,256]{1,0:T(8,128)(2,1)} %cotangent.1, ...), custom_call_target="tpu_custom_call" | custom-call | tf_op jit(solution)/shard_map/pallas_call | solution.py:445
  95.4 0.0 copy-start.1
  95.5 0.0 copy-start
  95.5 12.4 %shard_map.68 = f32[2,128,64,256]{3,2,1,0:T(8,128)} custom-call(f32[256,256]{1,0:T(8,128)} %get-tuple-element.9.x_real.x_imag, f32[256,256]{1,0:T(8,128)} %get-tuple-element.9.x_real.x_imag, f32[256,256]{1,0:T(8,128)} %get-tuple-element.10.g_real.g_imag, f32[256,256]{1,0:T(8,128)} %get-tuple-element.10.g_real.g_imag), custom_call_target="tpu_custom_call" | custom-call | tf_op jit(solution)/shard_map/pallas_call | solution.py:421
  107.9 0.0 copy-done.1
  107.9 0.9 copy.9
  108.8 0.0 copy-done
  108.8 0.9 copy.10
  (3 shorter events, 0.0 us)
Async XLA Ops:
  95.4 12.4 %copy-start.1 = (bf16[1536,256]{1,0:T(8,128)(2,1)S(1)}, bf16[1536,256]{1,0:T(8,128)(2,1)}, u32[]{:S(2)}) copy-start(bf16[1536,256]{1,0:T(8,128)(2,1)} %get-tuple-element.18) | copy-start | bytes 2359300
  95.5 13.3 %copy-start = (bf16[1536,256]{1,0:T(8,128)(2,1)S(1)}, bf16[1536,256]{1,0:T(8,128)(2,1)}, u32[]{:S(2)}) copy-start(bf16[1536,256]{1,0:T(8,128)(2,1)} %get-tuple-element.19) | copy-start | bytes 2359300

commit v2 on v1

--- a/solution.py
+++ b/solution.py
@@ -10,6 +10,7 @@
 
 LANES = 128
 FINE = 16
+PIECE_MODES = 64
 MODES_PER_STEP = 8
 VMEM_BYTES = 56 * 1024 * 1024
 F32 = jnp.float32
@@ -18,10 +19,12 @@
 
 def base_tables(mode_index, first_step, device_count, time_total):
     owned = mode_index.shape[0] // device_count
-    frequency = mode_index.reshape(device_count, 1, owned)
-    frequency = jnp.broadcast_to(frequency, (device_count, 2, owned)).reshape(1, -1)
+    depth = min(owned, PIECE_MODES)
+    frequency = mode_index.reshape(-1, 1, depth)
+    shape = (frequency.shape[0], 2, depth)
+    frequency = jnp.broadcast_to(frequency, shape).reshape(1, -1)
     quarter = jnp.arange(2, dtype=jnp.int32).reshape(1, 2, 1) * (time_total // 4)
-    quarter = jnp.broadcast_to(quarter, (device_count, 2, owned)).reshape(1, -1)
+    quarter = jnp.broadcast_to(quarter, shape).reshape(1, -1)
     row = jnp.arange(32, dtype=jnp.int32)
     steps = jnp.where(row < FINE, row, (row - FINE) * FINE)
     steps = jnp.where(row == 24, first_step, steps)
@@ -77,9 +80,9 @@
 def block_masks(block_size, width):
     row = lax.broadcasted_iota(jnp.int32, (block_size, width), 0)
     column = lax.broadcasted_iota(jnp.int32, (block_size, width), 1)
-    pick = column % block_size == row
-    left = lax.broadcasted_iota(jnp.int32, (width, width), 0) // block_size
-    right = lax.broadcasted_iota(jnp.int32, (width, width), 1) // block_size
+    pick = lax.rem(column, block_size) == row
+    left = lax.div(lax.broadcasted_iota(jnp.int32, (width, width), 0), block_size)
+    right = lax.div(lax.broadcasted_iota(jnp.int32, (width, width), 1), block_size)
     return pick, (left == right).astype(F32).astype(BF16)
 
 
@@ -99,6 +102,19 @@
 
 def fold(values, block_size):
     return values.reshape(MODES_PER_STEP, block_size, values.shape[1]).sum(axis=1)
+
+
+def loop(begin, end, step):
+    if end - begin <= 8:
+        for k in range(begin, end):
+            step(k)
+    else:
+
+        def one(k, carry):
+            step(k)
+            return carry
+
+        lax.fori_loop(begin, end, one, 0)
 
 
 def mode_weights(weight, part, first_row):
@@ -146,13 +162,24 @@
     owned = weight.shape[1]
     block_size = weight.shape[2]
     rows = 2 * owned
+    depth = min(owned, PIECE_MODES)
+    pieces = owned // depth
+    piece_rows = 2 * depth
     time_rows, width = series.shape
     me = lax.axis_index("tm")
-    high, low = me // 2, me % 2
+    high, low = lax.div(me, 2), lax.rem(me, 2)
     partner = high * 2 + 1 - low
 
     def peer(offset):
         return lax.rem(high + offset, half) * 2 + low
+
+    def offset_of(k):
+        if half != 4:
+            return k + 1
+        return (2, 1, 3, 4)[k]
+
+    def piece(device, q):
+        return pl.ds(pl.multiple_of(device * rows + q * piece_rows, piece_rows), piece_rows)
 
     def block(device):
         return pl.ds(pl.multiple_of(device * rows, rows), rows)
@@ -178,76 +205,137 @@
 
     lax.fori_loop(1, half, greet, 0)
 
-    def reduce_scatter(phase, signal, factor, meanwhile):
-        def pair_copy(k):
-            target = lax.rem(high + 1 + k, half) * 2 + 1 - low
-            return copy(
-                partial.at[phase, block(target)],
-                pair_in.at[phase, k],
-                pair_send.at[phase, k],
-                pair_recv.at[phase, k],
-                partner,
-            )
-
-        def line_copy(k):
-            return copy(
-                pair_sum.at[phase, k],
-                line_in.at[phase, k],
-                line_send.at[phase, k],
-                line_recv.at[phase, k],
-                peer(k + 1),
-            )
-
+    def pair_target(k):
+        return lax.rem(high + offset_of(k), half) * 2 + 1 - low
+
+    def pair_copy(phase, q, k):
+        return copy(
+            partial.at[phase, piece(pair_target(k), q)],
+            pair_in.at[phase, q, k],
+            pair_send.at[phase, q, k],
+            pair_recv.at[phase, q, k],
+            partner,
+        )
+
+    def line_copy(phase, q, k):
+        return copy(
+            pair_sum.at[phase, q, k],
+            line_in.at[phase, q, k],
+            line_send.at[phase, q, k],
+            line_recv.at[phase, q, k],
+            peer(offset_of(k)),
+        )
+
+    def share_copy(phase, q, k):
+        mine = gathered.at[phase, piece(me, q)]
+        return copy(mine, mine, share_send.at[phase, q, k], share_recv.at[phase, q, k], peer(k))
+
+    def cross_copy(phase, q, k):
+        held = gathered.at[phase, piece(lax.rem(high - k + half, half) * 2 + low, q)]
+        return copy(held, held, cross_send.at[phase, q, k], cross_recv.at[phase, q, k], partner)
+
+    def arrival(phase, device, q, recv_sem):
+        place = gathered.at[phase, piece(device, q)]
+        return copy(place, place, recv_sem, recv_sem, partner)
+
+    def exchange(phase, signal, factor, mode_step, meanwhile):
         def project(device):
             product = jnp.dot(table_t[block(device), :], signal[...], preferred_element_type=F32)
             partial[phase, block(device), :] = (product * factor).astype(BF16)
 
-        def send_pair(k, carry):
-            project(lax.rem(high + 1 + k, half) * 2 + 1 - low)
-            pair_copy(k).start()
-            return carry
-
-        lax.fori_loop(0, half, send_pair, 0)
-
-        def own_part(k, carry):
-            project(peer(k + 1))
-            return carry
-
-        lax.fori_loop(0, half, own_part, 0)
-
-        def send_line(k, carry):
-            pair_copy(k).wait_recv()
-            own = partial[phase, block(peer(k + 1)), :].astype(F32)
-            pair_sum[phase, k] = (own + pair_in[phase, k].astype(F32)).astype(BF16)
-            line_copy(k).start()
-            return carry
-
-        lax.fori_loop(0, half - 1, send_line, 0)
-        meanwhile()
-        pair_copy(half - 1).wait_recv()
-        total = partial[phase, block(me), :].astype(F32) + pair_in[phase, half - 1].astype(F32)
-
-        def add(k, total):
-            line_copy(k).wait_recv()
-            return total + line_in[phase, k].astype(F32)
-
-        for k in range(half - 1) if half <= 8 else ():
-            total = add(k, total)
-        if half > 8:
-            total = lax.fori_loop(0, half - 1, add, total)
-        spectrum[phase] = total.astype(BF16).astype(F32)
-
-        def done(k, carry):
-            pair_copy(k).wait_send()
-            return carry
-
-        lax.fori_loop(0, half, done, 0)
-
-        def done_line(k, carry):
-            line_copy(k).wait_send()
-            return carry
-
-        lax.fori_loop(0, half - 1, done_line, 0)
+        def send_first(k):
+            project(pair_target(k))
+            pair_copy(phase, 0, k).start()
+
+        def forward(q):
+            def one(k):
+                device = lax.rem(high - k + half, half) * 2 + low
+                arrival(phase, device, q, share_recv.at[phase, q, k]).wait_recv()
+                cross_copy(phase, q, k).start()
+
+            loop(1, half, one)
+
+        def line_piece(q):
+            def send_line(k):
+                pair_copy(phase, q, k).wait_recv()
+                own = partial[phase, piece(peer(offset_of(k)), q), :].astype(F32)
+                pair_sum[phase, q, k] = (own + pair_in[phase, q, k].astype(F32)).astype(BF16)
+                line_copy(phase, q, k).start()
+
+            loop(0, half - 1, send_line)
+
+        def mix_piece(q):
+            place = pl.ds(q * piece_rows, piece_rows)
+            pair_copy(phase, q, half - 1).wait_recv()
+            spectrum[phase, place, :] = (
+                partial[phase, piece(me, q), :].astype(F32) + pair_in[phase, q, half - 1].astype(F32)
+            )
+
+            def add(k):
+                line_copy(phase, q, k).wait_recv()
+                spectrum[phase, place, :] += line_in[phase, q, k].astype(F32)
+
+            loop(0, half - 1, add)
+            spectrum[phase, place, :] = spectrum[phase, place, :].astype(BF16).astype(F32)
+            if phase == 0 and q == 0:
+                load.wait()
+
+            def mode_steps(step, carry):
+                first = pl.multiple_of(q * piece_rows + step * MODES_PER_STEP, MODES_PER_STEP)
+                mode_step(first, first + depth, pl.multiple_of(q * depth + step * MODES_PER_STEP, MODES_PER_STEP))
+                return carry
+
+            lax.fori_loop(0, depth // MODES_PER_STEP, mode_steps, 0)
+            gathered[phase, piece(me, q), :] = rows_out[place, :].astype(BF16)
+            loop(1, half, lambda k: share_copy(phase, q, k).start())
+            cross_copy(phase, q, 0).start()
+
+        loop(0, half, send_first)
+        for q in range(1, pieces):
+            loop(0, half, lambda k: pair_copy(phase, q, k).start())
+        loop(0, half, lambda k: project(peer(offset_of(k))))
+        for q in range(pieces):
+            line_piece(q)
+            if q == 0:
+                meanwhile()
+            if q > 0:
+                mix_piece(q - 1)
+            if q > 1:
+                forward(q - 2)
+        mix_piece(pieces - 1)
+        if pieces > 1:
+            forward(pieces - 2)
+        early = rows % LANES == 0
+        if early:
+            add_block(phase, me * rows, rows, True)
+        forward(pieces - 1)
+        if early:
+            loop(1, half, lambda k: add_block(phase, (lax.rem(high - k + half, half) * 2 + low) * rows, rows, False))
+
+        def receive(k):
+            device = lax.rem(high - k + half, half) * 2 + 1 - low
+            for q in range(pieces):
+                arrival(phase, device, q, cross_recv.at[phase, q, k]).wait_recv()
+            if early:
+                add_block(phase, device * rows, rows, False)
+
+        loop(0, half, receive)
+        if not early:
+            add_block(phase, 0, 2 * LANES, True)
+            loop(1, count * rows // (2 * LANES), lambda u: add_block(phase, u * 2 * LANES, 2 * LANES, False))
+
+        def sent(k):
+            for q in range(pieces):
+                pair_copy(phase, q, k).wait_send()
+                cross_copy(phase, q, k).wait_send()
+
+        def sent_line(k):
+            for q in range(pieces):
+                line_copy(phase, q, k).wait_send()
+                share_copy(phase, q, k + 1).wait_send()
+
+        loop(0, half, sent)
+        loop(0, half - 1, sent_line)
 
     def add_block(phase, first_row, depth, begin):
         place = pl.ds(pl.multiple_of(first_row, depth), depth)
@@ -264,97 +352,19 @@
 
         lax.fori_loop(0, time_rows // (2 * LANES), tile, 0)
 
-    def gather(phase):
-        early = rows % LANES == 0
-
-        def share_copy(k):
-            return copy(
-                gathered.at[phase, block(me)],
-                gathered.at[phase, block(me)],
-                share_send.at[phase, k],
-                share_recv.at[phase, k],
-                peer(k),
-            )
-
-        def cross_copy(k):
-            held = block(lax.rem(high - k + half, half) * 2 + low)
-            return copy(
-                gathered.at[phase, held],
-                gathered.at[phase, held],
-                cross_send.at[phase, k],
-                cross_recv.at[phase, k],
-                partner,
-            )
-
-        def arrival(device, recv_sem):
-            place = gathered.at[phase, block(device)]
-            return copy(place, place, recv_sem, recv_sem, partner)
-
-        gathered[phase, block(me), :] = rows_out[...].astype(BF16)
-        cross_copy(0).start()
-
-        def share(k, carry):
-            share_copy(k).start()
-            return carry
-
-        lax.fori_loop(1, half, share, 0)
-        if early:
-            add_block(phase, me * rows, rows, True)
-
-        def forward(k, carry):
-            device = lax.rem(high - k + half, half) * 2 + low
-            arrival(device, share_recv.at[phase, k]).wait_recv()
-            cross_copy(k).start()
-            if early:
-                add_block(phase, device * rows, rows, False)
-            return carry
-
-        lax.fori_loop(1, half, forward, 0)
-
-        def receive(k, carry):
-            device = lax.rem(high - k + half, half) * 2 + 1 - low
-            arrival(device, cross_recv.at[phase, k]).wait_recv()
-            if early:
-                add_block(phase, device * rows, rows, False)
-            return carry
-
-        lax.fori_loop(0, half, receive, 0)
-        if not early:
-            depth = 2 * LANES
-            add_block(phase, 0, depth, True)
-
-            def rest(unit, carry):
-                add_block(phase, unit * depth, depth, False)
-                return carry
-
-            lax.fori_loop(1, count * rows // depth, rest, 0)
-
-        def done(k, carry):
-            share_copy(k).wait_send()
-            cross_copy(k).wait_send()
-            return carry
-
-        lax.fori_loop(1, half, done, 0)
-        cross_copy(0).wait_send()
-
     pick, same_block = block_masks(block_size, width)
 
-    def mix(step, carry):
-        first = pl.multiple_of(step * MODES_PER_STEP, MODES_PER_STEP)
-        second = pl.multiple_of(owned + step * MODES_PER_STEP, MODES_PER_STEP)
+    def mix(first, second, mode):
         x_real = expand(spectrum.at[0], first, pick, same_block)
         x_imag = expand(spectrum.at[0], second, pick, same_block)
-        w_real, w_imag = mode_weights(weight, 0, first), mode_weights(weight, 1, first)
+        w_real, w_imag = mode_weights(weight, 0, mode), mode_weights(weight, 1, mode)
         rows_out[pl.ds(first, MODES_PER_STEP), :] = fold(x_real * w_real - x_imag * w_imag, block_size)
         rows_out[pl.ds(second, MODES_PER_STEP), :] = fold(x_real * w_imag + x_imag * w_real, block_size)
-        return carry
-
-    def mix_back(step, carry):
-        first = pl.multiple_of(step * MODES_PER_STEP, MODES_PER_STEP)
-        second = pl.multiple_of(owned + step * MODES_PER_STEP, MODES_PER_STEP)
+
+    def mix_back(first, second, mode):
         g_real = spread_rows(spectrum.at[1], first, block_size)
         g_imag = spread_rows(spectrum.at[1], second, block_size)
-        w_real, w_imag = mode_weights(weight, 0, first), mode_weights(weight, 1, first)
+        w_real, w_imag = mode_weights(weight, 0, mode), mode_weights(weight, 1, mode)
         chosen = jnp.concatenate([pick] * MODES_PER_STEP, axis=0)
 
         def gathered_rows(values):
@@ -363,14 +373,10 @@
 
         rows_out[pl.ds(first, MODES_PER_STEP), :] = gathered_rows(w_real * g_real + w_imag * g_imag)
         rows_out[pl.ds(second, MODES_PER_STEP), :] = gathered_rows(w_real * g_imag - w_imag * g_real)
-        return carry
 
     fill_tables(cos_ref, sin_ref, None, table_t)
     pl.semaphore_wait(barrier, half)
-    reduce_scatter(0, series, scale_in, lambda: fill_tables(cos_ref, sin_ref, table, None))
-    load.wait()
-    lax.fori_loop(0, owned // MODES_PER_STEP, mix, 0)
-    gather(0)
+    exchange(0, series, scale_in, mix, lambda: fill_tables(cos_ref, sin_ref, table, None))
 
     slope = math.sqrt(2.0 / math.pi)
 
@@ -389,11 +395,9 @@
         return carry
 
     lax.fori_loop(0, time_rows // LANES, activate, 0)
-    reduce_scatter(1, grad_low, scale_out, lambda: None)
-    lax.fori_loop(0, owned // MODES_PER_STEP, mix_back, 0)
+    exchange(1, grad_low, scale_out, mix_back, lambda: None)
     spectrum_out[...] = spectrum[0]
     grad_out[...] = spectrum[1]
-    gather(1)
 
     def finish(t, carry):
         steps = pl.ds(pl.multiple_of(t * LANES, LANES), LANES)
@@ -403,9 +407,16 @@
     lax.fori_loop(0, time_rows // LANES, finish, 0)
 
 
-def weight_grad_kernel(x_real, x_imag, g_real, g_imag, out):
+def weight_grad_kernel(x_real, x_imag, g_real, g_imag, out, pick_ref, same_ref):
     block_size, width = out.shape[2], out.shape[3]
-    pick, same_block = block_masks(block_size, width)
+
+    @pl.when(pl.program_id(0) == 0)
+    def _():
+        pick, same_block = block_masks(block_size, width)
+        pick_ref[...] = pick.astype(F32)
+        same_ref[...] = same_block
+
+    pick, same_block = pick_ref[...] > 0.5, same_ref[...]
     shape = (MODES_PER_STEP, block_size, width)
     xr, xi = expand(x_real, 0, pick, same_block), expand(x_imag, 0, pick, same_block)
     gr, gi = spread_rows(g_real, 0, block_size), spread_rows(g_imag, 0, block_size)
@@ -416,14 +427,20 @@
 def weight_gradient(spectrum, grad, block_size):
     owned, width = spectrum.shape[0] // 2, spectrum.shape[1]
     steps = owned // MODES_PER_STEP
-    real = pl.BlockSpec((MODES_PER_STEP, width), lambda g: (g, 0))
-    imag = pl.BlockSpec((MODES_PER_STEP, width), lambda g: (g + steps, 0))
+    per_piece = min(owned, PIECE_MODES) // MODES_PER_STEP
+
+    def place(part):
+        return lambda g: (g // per_piece * (2 * per_piece) + part * per_piece + g % per_piece, 0)
+
+    real = pl.BlockSpec((MODES_PER_STEP, width), place(0))
+    imag = pl.BlockSpec((MODES_PER_STEP, width), place(1))
     return pl.pallas_call(
         weight_grad_kernel,
         grid=(steps,),
         in_specs=[real, imag, real, imag],
         out_specs=pl.BlockSpec((2, MODES_PER_STEP, block_size, width), lambda g: (0, g, 0, 0)),
         out_shape=jax.ShapeDtypeStruct((2, owned, block_size, width), F32),
+        scratch_shapes=[pltpu.VMEM((block_size, width), F32), pltpu.VMEM((width, width), BF16)],
         compiler_params=pltpu.CompilerParams(vmem_limit_bytes=VMEM_BYTES),
     )(spectrum, spectrum, grad, grad)
 
@@ -435,13 +452,14 @@
     owned = mix_weight.shape[1]
     rows = 2 * owned
     half = count // 2
+    pieces = max(1, owned // PIECE_MODES)
     time_total = time_rows * count
     cos_base, sin_base = base_tables(mode_index, lax.axis_index("tm") * time_rows, count, time_total)
     kernel = functools.partial(
         spectral_kernel, 1.0 / math.sqrt(time_total), math.sqrt(2.0 / modes), count
     )
     vmem = pl.BlockSpec(memory_space=pltpu.VMEM)
-    sems = pltpu.SemaphoreType.DMA((2, half))
+    sems = pltpu.SemaphoreType.DMA((2, pieces, half))
     activated, series_grad, spectrum, grad = pl.pallas_call(
         kernel,
         in_specs=[vmem] * 4 + [pl.BlockSpec(memory_space=pl.ANY)],
@@ -460,9 +478,9 @@
             pltpu.VMEM((time_rows, width), F32),
             pltpu.VMEM((time_rows, width), BF16),
             pltpu.VMEM((2, 2 * modes, width), BF16),
-            pltpu.VMEM((2, half, rows, width), BF16),
-            pltpu.VMEM((2, half, rows, width), BF16),
-            pltpu.VMEM((2, half, rows, width), BF16),
+            pltpu.VMEM((2, pieces, half, rows // pieces, width), BF16),
+            pltpu.VMEM((2, pieces, half, rows // pieces, width), BF16),
+            pltpu.VMEM((2, pieces, half, rows // pieces, width), BF16),
             pltpu.VMEM((2, 2 * modes, width), BF16),
             pltpu.VMEM((2, rows, width), F32),
             pltpu.VMEM((rows, width), F32),

time: 111 us -> 101 us (0.910)
  Pallas kernels: 104 us -> 94 us
    pallas_call x1, Pallas kernels: 91.6 us -> 81.5 us  [body(): pl.pallas_call(kernel, in_specs=[vmem] * 4 + [pl.BlockSpec(memory_space=p...]
where the time goes in v2:
time: 101 us; the launch traced here: 99.8 us
  Pallas kernels  94 us (93%)
  local copies, waits for them, and re-layouts  2.77 us (3%)
  other arithmetic  2.4 us (2%)
    pallas_call x1, Pallas kernels, body(): pl.pallas_call(kernel, in_specs=[vmem] * 4 + [pl.BlockSpec(memory_space=p...  81.5 us
    pallas_call x1, Pallas kernels, weight_gradient(): pl.pallas_call(weight_grad_kernel, grid=(steps,), in_specs=[real, imag, r...  12.5 us
    sin x1, other arithmetic, base_tables(): return (jnp.cos(angle), jnp.sin(angle))  2.37 us

profile of v2, /device:TPU:0, one launch (start us, length us, event | category | flops | bytes accessed | tf_op | source)
XLA Modules:
  0.0 99.8 jit_solution(18375271330896953155)
XLA Ops:
  0.7 0.8 broadcast_in_dim.49
  1.4 0.1 mul.59
  1.5 0.1 broadcast_in_dim.56
  1.6 0.1 broadcast_in_dim.57
  1.7 2.4 %fusion.16 = (f32[32,2048]{1,0:T(8,128)}, f32[32,2048]{1,0:T(8,128)}) fusion(s32[2048]{0:T(1024)S(1)} %broadcast_in_dim.57, pred[32]{0:T(512)(128)(4,1)S(1)} %compare_or_fusion, s32[32]{0:T(128)S(1)} %get-tuple-element.13, s32[32]{0:T(128)S(1)} %get-tuple-element.14, s32[2048]{0:T(1024)S(1)} %mul.59), kind=kLoop, calls=%fused_computation.22 | loop fusion | flops 2097152 | bytes 540960 | tf_op jit(solution)/shard_map/sin | solution.py:39
  4.1 81.5 %shard_map.67 = (bf16[1536,256]{1,0:T(8,128)(2,1)}, bf16[1536,256]{1,0:T(8,128)(2,1)}, f32[256,256]{1,0:T(8,128)}, f32[256,256]{1,0:T(8,128)}) custom-call(f32[32,2048]{1,0:T(8,128)} %get-tuple-element.12.cos_ref, f32[32,2048]{1,0:T(8,128)} %get-tuple-element.11.sin_ref, bf16[1536,256]{1,0:T(8,128)(2,1)} %series.1, bf16[1536,256]{1,0:T(8,128)(2,1)} %cotangent.1, ...), custom_call_target="tpu_custom_call" | custom-call | tf_op jit(solution)/shard_map/pallas_call | solution.py:463
  85.6 0.0 copy-start.1
  85.6 0.0 copy-start
  85.6 12.5 %shard_map.68 = f32[2,128,64,256]{3,2,1,0:T(8,128)} custom-call(f32[256,256]{1,0:T(8,128)} %get-tuple-element.9.x_real.x_imag, f32[256,256]{1,0:T(8,128)} %get-tuple-element.9.x_real.x_imag, f32[256,256]{1,0:T(8,128)} %get-tuple-element.10.g_real.g_imag, f32[256,256]{1,0:T(8,128)} %get-tuple-element.10.g_real.g_imag), custom_call_target="tpu_custom_call" | custom-call | tf_op jit(solution)/shard_map/pallas_call | solution.py:437
  98.1 0.0 copy-done.1
  98.1 0.9 copy.9
  99.0 0.0 copy-done
  99.0 0.9 copy.10
  (4 shorter events, 0.0 us)
Async XLA Ops:
  85.6 12.5 %copy-start.1 = (bf16[1536,256]{1,0:T(8,128)(2,1)S(1)}, bf16[1536,256]{1,0:T(8,128)(2,1)}, u32[]{:S(2)}) copy-start(bf16[1536,256]{1,0:T(8,128)(2,1)} %get-tuple-element.18) | copy-start | bytes 2359300
  85.6 13.4 %copy-start = (bf16[1536,256]{1,0:T(8,128)(2,1)S(1)}, bf16[1536,256]{1,0:T(8,128)(2,1)}, u32[]{:S(2)}) copy-start(bf16[1536,256]{1,0:T(8,128)(2,1)} %get-tuple-element.19) | copy-start | bytes 2359300

commit v3 on v2

--- a/solution.py
+++ b/solution.py
@@ -11,6 +11,7 @@
 LANES = 128
 FINE = 16
 PIECE_MODES = 64
+WG_MODES = 32
 MODES_PER_STEP = 8
 VMEM_BYTES = 56 * 1024 * 1024
 F32 = jnp.float32
@@ -417,28 +418,33 @@
         same_ref[...] = same_block
 
     pick, same_block = pick_ref[...] > 0.5, same_ref[...]
-    shape = (MODES_PER_STEP, block_size, width)
-    xr, xi = expand(x_real, 0, pick, same_block), expand(x_imag, 0, pick, same_block)
-    gr, gi = spread_rows(g_real, 0, block_size), spread_rows(g_imag, 0, block_size)
-    out[0] = (xr * gr + xi * gi).reshape(shape)
-    out[1] = (xr * gi - xi * gr).reshape(shape)
+    spread = jnp.where(pick, 1.0, 0.0)
+
+    for mode in range(out.shape[1]):
+        row = slice(mode, mode + 1)
+        gr, gi = g_real[row, :], g_imag[row, :]
+        xr = jnp.dot((spread * x_real[row, :]).astype(BF16), same_block, preferred_element_type=F32)
+        xi = jnp.dot((spread * x_imag[row, :]).astype(BF16), same_block, preferred_element_type=F32)
+        out[0, mode] = xr * gr + xi * gi
+        out[1, mode] = xr * gi - xi * gr
 
 
 def weight_gradient(spectrum, grad, block_size):
     owned, width = spectrum.shape[0] // 2, spectrum.shape[1]
-    steps = owned // MODES_PER_STEP
-    per_piece = min(owned, PIECE_MODES) // MODES_PER_STEP
+    step_modes = min(owned, WG_MODES)
+    steps = owned // step_modes
+    per_piece = min(owned, PIECE_MODES) // step_modes
 
     def place(part):
         return lambda g: (g // per_piece * (2 * per_piece) + part * per_piece + g % per_piece, 0)
 
-    real = pl.BlockSpec((MODES_PER_STEP, width), place(0))
-    imag = pl.BlockSpec((MODES_PER_STEP, width), place(1))
+    real = pl.BlockSpec((step_modes, width), place(0))
+    imag = pl.BlockSpec((step_modes, width), place(1))
     return pl.pallas_call(
         weight_grad_kernel,
         grid=(steps,),
         in_specs=[real, imag, real, imag],
-        out_specs=pl.BlockSpec((2, MODES_PER_STEP, block_size, width), lambda g: (0, g, 0, 0)),
+        out_specs=pl.BlockSpec((2, step_modes, block_size, width), lambda g: (0, g, 0, 0)),
         out_shape=jax.ShapeDtypeStruct((2, owned, block_size, width), F32),
         scratch_shapes=[pltpu.VMEM((block_size, width), F32), pltpu.VMEM((width, width), BF16)],
         compiler_params=pltpu.CompilerParams(vmem_limit_bytes=VMEM_BYTES),

time: 101 us -> 97.4 us (0.964)
  Pallas kernels: 94 us -> 91.3 us
    pallas_call x1, Pallas kernels: 12.5 us -> 9.79 us  [weight_gradient(): pl.pallas_call(weight_grad_kernel, grid=(steps,), in_specs=[real, imag, r...]
where the time goes in v3:
time: 97.4 us; the launch traced here: 97.2 us
  Pallas kernels  91.3 us (94%)
  local copies, waits for them, and re-layouts  2.77 us (3%)
  other arithmetic  2.4 us (2%)
    pallas_call x1, Pallas kernels, body(): pl.pallas_call(kernel, in_specs=[vmem] * 4 + [pl.BlockSpec(memory_space=p...  81.5 us
    pallas_call x1, Pallas kernels, weight_gradient(): pl.pallas_call(weight_grad_kernel, grid=(steps,), in_specs=[real, imag, r...  9.79 us
    sin x1, other arithmetic, base_tables(): return (jnp.cos(angle), jnp.sin(angle))  2.37 us

profile of v3, /device:TPU:0, one launch (start us, length us, event | category | flops | bytes accessed | tf_op | source)
XLA Modules:
  0.0 97.2 jit_solution(1204590722222118685)
XLA Ops:
  0.7 0.8 broadcast_in_dim.49
  1.4 0.1 mul.59
  1.5 0.1 broadcast_in_dim.56
  1.6 0.1 broadcast_in_dim.57
  1.7 2.4 %fusion.16 = (f32[32,2048]{1,0:T(8,128)}, f32[32,2048]{1,0:T(8,128)}) fusion(s32[2048]{0:T(1024)S(1)} %broadcast_in_dim.57, pred[32]{0:T(512)(128)(4,1)S(1)} %compare_or_fusion, s32[32]{0:T(128)S(1)} %get-tuple-element.13, s32[32]{0:T(128)S(1)} %get-tuple-element.14, s32[2048]{0:T(1024)S(1)} %mul.59), kind=kLoop, calls=%fused_computation.22 | loop fusion | flops 2097152 | bytes 540960 | tf_op jit(solution)/shard_map/sin | solution.py:40
  4.1 81.5 %shard_map.67 = (bf16[1536,256]{1,0:T(8,128)(2,1)}, bf16[1536,256]{1,0:T(8,128)(2,1)}, f32[256,256]{1,0:T(8,128)}, f32[256,256]{1,0:T(8,128)}) custom-call(f32[32,2048]{1,0:T(8,128)} %get-tuple-element.12.cos_ref, f32[32,2048]{1,0:T(8,128)} %get-tuple-element.11.sin_ref, bf16[1536,256]{1,0:T(8,128)(2,1)} %series.1, bf16[1536,256]{1,0:T(8,128)(2,1)} %cotangent.1, ...), custom_call_target="tpu_custom_call" | custom-call | tf_op jit(solution)/shard_map/pallas_call | solution.py:469
  85.6 0.0 copy-start.1
  85.6 0.0 copy-start
  85.6 9.8 %shard_map.68 = f32[2,128,64,256]{3,2,1,0:T(8,128)} custom-call(f32[256,256]{1,0:T(8,128)} %get-tuple-element.9.x_real.x_imag, f32[256,256]{1,0:T(8,128)} %get-tuple-element.9.x_real.x_imag, f32[256,256]{1,0:T(8,128)} %get-tuple-element.10.g_real.g_imag, f32[256,256]{1,0:T(8,128)} %get-tuple-element.10.g_real.g_imag), custom_call_target="tpu_custom_call" | custom-call | tf_op jit(solution)/shard_map/pallas_call | solution.py:443
  95.4 0.0 copy-done.1
  95.4 0.9 copy.9
  96.3 0.0 copy-done
  96.3 0.9 copy.10
  (4 shorter events, 0.0 us)
Async XLA Ops:
  85.6 9.8 %copy-start.1 = (bf16[1536,256]{1,0:T(8,128)(2,1)S(1)}, bf16[1536,256]{1,0:T(8,128)(2,1)}, u32[]{:S(2)}) copy-start(bf16[1536,256]{1,0:T(8,128)(2,1)} %get-tuple-element.18) | copy-start | bytes 2359300
  85.6 10.7 %copy-start = (bf16[1536,256]{1,0:T(8,128)(2,1)S(1)}, bf16[1536,256]{1,0:T(8,128)(2,1)}, u32[]{:S(2)}) copy-start(bf16[1536,256]{1,0:T(8,128)(2,1)} %get-tuple-element.19) | copy-start | bytes 2359300
